TPU v7x, 32 devices: a whole 2x2x4 slice. The times are simulated.
32 devices in a mesh: groups: 2 (over y), dp: 4 (over z), mp: 2 (over x), section: 2 (over core).
Axes of the slice: x: 2, y: 2, z: 4, core: 2. Of those that a mesh axis runs over, the one named last changes fastest.
Arguments:
- online_obs: bfloat16 [64, 192, 2048], P('dp', 'groups', 'mp'), parts along dimension 1, may hold values from -6 to 6
- offline_obs: bfloat16 [64, 64, 2048], P(('groups', 'dp'), None, 'mp'), parts along dimension 0, may hold values from -6 to 6
- online_rewards: float32 [64, 192], P('dp', 'groups'), parts along dimension 1, may hold values from -6 to 6
- offline_rewards: float32 [64, 64], P(('groups', 'dp')), parts along dimension 0, may hold values from -6 to 6
- online_behaviour: float32 [64, 192], P('dp', 'groups'), parts along dimension 1, may hold values from -4.5 to -1.5
- offline_behaviour: float32 [64, 64], P(('groups', 'dp')), parts along dimension 0, may hold values from -4.5 to -1.5
- online_actions: int32 [64, 192], P('dp', 'groups'), parts along dimension 1, may hold values from 0 to 17
- offline_actions: int32 [64, 64], P(('groups', 'dp')), parts along dimension 0, may hold values from 0 to 17
- online_done: int32 [64, 192], P('dp', 'groups'), parts along dimension 1, may hold values 0 or 1
- offline_done: int32 [64, 64], P(('groups', 'dp')), parts along dimension 0, may hold values 0 or 1
- online_lengths: int32 [192], P(('groups', 'dp')), parts along dimension 0, may hold values from 16 to 64, as said below
- offline_lengths: int32 [64], P(('groups', 'dp')), parts along dimension 0, may hold values from 16 to 64, as said below
- torso_weights: bfloat16 [2, 2048, 2048], P('section', None, 'mp'), may hold values from -0.125 to 0.125
- value_head: bfloat16 [2048], P('mp'), may hold values from -0.125 to 0.125
- policy_head: bfloat16 [2048, 18], P('mp'), may hold values from -0.125 to 0.125
Outputs:
- torso_grads: float32 [4, 2048, 2048], P(('groups', 'section'), None, 'mp'), parts along dimension 0
There are 2 independent parts, one for each index of `groups`. A program takes and returns all parts, laid end to end along the dimension named above; an argument that names none is the same for every part. Nothing has to cross between parts.
Inputs may be any that keep to these rules, and one draw needn't show every extreme that they name: `online_lengths`: each array has a trajectory of full length 64. `offline_lengths`: each array has a trajectory of full length 64.
All inputs are finite; a program needn't handle non-finite values. No bound on the sum of `online_done` or of `offline_done` on one device may be relied on, other than what follows from the above.
Results may differ from a plain program's by a relative error of at most 0.003.
Values may be sent and summed in bfloat16 or wider, within the bound.
No kernel may reach another device: no remote copies, remote signals or barrier semaphores. Data moves between devices by JAX's collectives and lax.ppermute only.
A program may use at most 128 MiB of HBM per device.

v0:
```python
import math

import jax
import jax.numpy as jnp
from jax import lax
from jax.sharding import PartitionSpec as P

DISCOUNT_RATE = 0.99
TRACE_LAMBDA = 0.95


def silu_slope(pre):
    sigma = jax.nn.sigmoid(pre)
    return sigma * (1.0 + pre * (1.0 - sigma))


def importance_trace_terms(
    value_estimates,
    policy_logits,
    reward_rows,
    behaviour_probs,
    taken_actions,
    episode_finished,
    sequence_length,
    objective_scale,
):
    seq_count, step_count = value_estimates.shape
    action_count = policy_logits.shape[0]
    positions = jnp.arange(step_count, dtype=jnp.int32)
    valid_mask = (positions[None, :] < sequence_length[:, None]).astype(jnp.float32)
    zero_column = jnp.zeros((seq_count, 1), jnp.float32)
    valid_next = jnp.concatenate([valid_mask[:, 1:], zero_column], axis=1)
    log_probs = jax.nn.log_softmax(policy_logits, axis=0)
    one_hot = (
        jnp.arange(action_count, dtype=jnp.int32)[:, None, None] == taken_actions[None]
    ).astype(jnp.float32)
    chosen = jnp.sum(one_hot * log_probs, axis=0)
    clip_ratio = jnp.exp(jnp.minimum(chosen - behaviour_probs, 0.0))
    discount = DISCOUNT_RATE * (1.0 - episode_finished.astype(jnp.float32))
    next_value = jnp.concatenate([value_estimates[:, 1:], zero_column], axis=1) * valid_next
    td_error = valid_mask * clip_ratio * (reward_rows + discount * next_value - value_estimates)
    trace_coef = discount * TRACE_LAMBDA * clip_ratio * valid_next

    def backward_step(carried, inputs):
        error_now, coef_now = inputs
        updated = error_now + coef_now * carried
        return (updated, updated)

    final_state, stacked = lax.scan(
        backward_step,
        jnp.zeros((seq_count,), jnp.float32),
        (td_error.T, trace_coef.T),
        reverse=True,
    )
    correction = stacked.T
    targets = value_estimates + correction
    next_target = jnp.concatenate([targets[:, 1:], zero_column], axis=1) * valid_next
    policy_adv = clip_ratio * (reward_rows + discount * next_target - value_estimates)
    value_gradient = -objective_scale * valid_mask * correction
    logits_gradient = (
        objective_scale * (valid_mask * policy_adv)[None] * (jnp.exp(log_probs) - one_hot)
    )
    return (value_gradient, logits_gradient)


def head_terms(hidden, value_w, policy_w):
    logit_part = jnp.einsum("rh,ha->ar", hidden, policy_w, preferred_element_type=jnp.float32)
    value_part = jnp.dot(hidden, value_w, preferred_element_type=jnp.float32)
    return jnp.concatenate([logit_part, value_part[None]], axis=0)


def full_rows(online_part, offline_part):
    return (
        lax.all_gather(online_part, "mp", axis=2, tiled=True),
        lax.all_gather(offline_part, "mp", axis=2, tiled=True),
    )


def per_device(
    online_obs,
    offline_obs,
    online_rewards,
    offline_rewards,
    online_behaviour,
    offline_behaviour,
    online_actions,
    offline_actions,
    online_done,
    offline_done,
    online_lengths,
    offline_lengths,
    torso_weights,
    value_head,
    policy_head,
):
    owned_online = online_lengths.shape[0]
    owned_offline = offline_obs.shape[0]
    step_count = offline_obs.shape[1]
    action_count = policy_head.shape[1]
    record_stack = jnp.stack(
        [
            online_rewards,
            online_behaviour,
            online_actions.astype(jnp.float32),
            online_done.astype(jnp.float32),
        ]
    )
    records = lax.all_to_all(record_stack, "dp", split_axis=2, concat_axis=1, tiled=True)
    slabs = lax.all_to_all(online_obs, "dp", split_axis=1, concat_axis=0, tiled=True)
    x_online, x_offline = full_rows(slabs, offline_obs)
    feature_count = x_online.shape[2]
    x_online = x_online.reshape(step_count * owned_online, feature_count)
    x_offline = x_offline.reshape(owned_offline * step_count, feature_count)
    weight = torso_weights[0]
    pre_online = jnp.dot(x_online, weight, preferred_element_type=jnp.float32)
    pre_offline = jnp.dot(x_offline, weight, preferred_element_type=jnp.float32)
    hidden_online = jax.nn.silu(pre_online).astype(jnp.bfloat16)
    hidden_offline = jax.nn.silu(pre_offline).astype(jnp.bfloat16)
    is_critic = (lax.axis_index("section") == 0).astype(jnp.float32)
    is_policy = 1.0 - is_critic
    row_keep = jnp.where(jnp.arange(action_count + 1) == action_count, is_critic, is_policy)
    partial_value = jnp.concatenate(
        [
            head_terms(hidden_online, value_head, policy_head),
            head_terms(hidden_offline, value_head, policy_head),
        ],
        axis=1,
    )
    partial_value = partial_value * row_keep[:, None]
    heads = lax.psum(partial_value, ("mp", "section"))
    online_count = step_count * owned_online
    logits_on = (
        heads[:action_count, :online_count]
        .reshape(action_count, step_count, owned_online)
        .transpose(0, 2, 1)
    )
    logits_off = heads[:action_count, online_count:].reshape(
        action_count, owned_offline, step_count
    )
    values_on = heads[action_count, :online_count].reshape(step_count, owned_online).T
    values_off = heads[action_count, online_count:].reshape(owned_offline, step_count)
    record_seq = records.transpose(0, 2, 1)
    value_estimates = jnp.concatenate([values_on, values_off], axis=0)
    policy_logits = jnp.concatenate([logits_on, logits_off], axis=1)
    reward_rows = jnp.concatenate([record_seq[0], offline_rewards], axis=0)
    behaviour_probs = jnp.concatenate([record_seq[1], offline_behaviour], axis=0)
    taken_actions = jnp.concatenate([record_seq[2].astype(jnp.int32), offline_actions], axis=0)
    episode_finished = jnp.concatenate([record_seq[3].astype(jnp.int32), offline_done], axis=0)
    sequence_length = jnp.concatenate([online_lengths, offline_lengths], axis=0)
    total_seqs = online_obs.shape[1] + owned_offline * lax.axis_size("dp")
    hidden_total = value_head.shape[0] * lax.axis_size("mp")
    objective_scale = math.sqrt(hidden_total / (total_seqs * step_count))
    value_gradient, logits_gradient = importance_trace_terms(
        value_estimates,
        policy_logits,
        reward_rows,
        behaviour_probs,
        taken_actions,
        episode_finished,
        sequence_length,
        objective_scale,
    )
    value_gradient = value_gradient * is_critic
    logits_gradient = logits_gradient * is_policy
    dv_on = value_gradient[:owned_online].T.reshape(online_count)
    dv_off = value_gradient[owned_online:].reshape(owned_offline * step_count)
    dl_on = logits_gradient[:, :owned_online].transpose(0, 2, 1).reshape(action_count, online_count)
    dl_off = logits_gradient[:, owned_online:].reshape(action_count, owned_offline * step_count)
    value_w = value_head.astype(jnp.float32)
    policy_w = policy_head.astype(jnp.float32)
    dh_on = dv_on[:, None] * value_w[None, :] + jnp.einsum(
        "ar,ha->rh", dl_on, policy_w, precision=lax.Precision.HIGHEST
    )
    dh_off = dv_off[:, None] * value_w[None, :] + jnp.einsum(
        "ar,ha->rh", dl_off, policy_w, precision=lax.Precision.HIGHEST
    )
    dz_online = (dh_on * silu_slope(pre_online)).astype(jnp.bfloat16)
    dz_offline = (dh_off * silu_slope(pre_offline)).astype(jnp.bfloat16)
    local_grad = jnp.einsum("rd,rh->dh", x_online, dz_online, preferred_element_type=jnp.float32)
    local_grad = local_grad + jnp.einsum(
        "rd,rh->dh", x_offline, dz_offline, preferred_element_type=jnp.float32
    )
    summed = lax.psum(local_grad, "dp")
    return summed[None]


def solution(mesh):
    in_specs = (
        P("dp", "groups", "mp"),
        P(("groups", "dp"), None, "mp"),
        P("dp", "groups"),
        P(("groups", "dp"), None),
        P("dp", "groups"),
        P(("groups", "dp"), None),
        P("dp", "groups"),
        P(("groups", "dp"), None),
        P("dp", "groups"),
        P(("groups", "dp"), None),
        P(("groups", "dp")),
        P(("groups", "dp")),
        P("section", None, "mp"),
        P("mp"),
        P("mp", None),
    )
    out_specs = P(("groups", "section"), None, "mp")
    return jax.shard_map(
        per_device, mesh=mesh, in_specs=in_specs, out_specs=out_specs, check_vma=False
    )
```

profile of v0, /device:TPU:0, one launch (start us, length us, event | category | flops | bytes accessed | tf_op | source)
XLA Modules:
  0.0 560.9 jit_solution(10728846152969824006)
XLA Ops:
  6.5 5.3 copy.65
  11.8 6.3 %all-to-all-start.1 = ((bf16[16,96,1024]{2,0,1:T(8,128)(2,1)}), bf16[16,96,1024]{2,0,1:T(8,128)(2,1)S(1)}, u32[]{:S(2)}, u32[]{:S(2)}) async-start(bf16[16,96,1024]{2,0,1:T(8,128)(2,1)} %copy.65), calls=%async_computation.1 | async-start | bytes 6291456 | tf_op jit(solution)/shard_map/all_to_all | solution.py:109
  18.1 0.7 all-gather.5.cloned.1.call-update
  18.9 69.9 %all-to-all-done.1 = bf16[16,96,1024]{2,0,1:T(8,128)(2,1)S(1)} async-done(((bf16[16,96,1024]{2,0,1:T(8,128)(2,1)}), bf16[16,96,1024]{2,0,1:T(8,128)(2,1)S(1)}, u32[]{:S(2)}, u32[]{:S(2)}) %all-to-all-start.1) | async-done | bytes 3145760 | tf_op jit(solution)/shard_map/all_to_all | solution.py:109
  88.8 3.4 copy.67
  92.4 0.6 copy-done.3
  93.1 0.8 reshape.56
  93.9 3.3 all-to-all-start
  97.8 5.0 all-to-all-done
  102.8 0.5 broadcast.71
  103.3 0.6 reduce.6
  104.3 7.3 %multiply_convert_fusion.3 = (bf16[512,1024]{1,0:T(8,128)(2,1)S(1)}, f32[512,1024]{1,0:T(8,128)}) fusion(bf16[512,2048]{1,0:T(8,128)(2,1)} %bitcast.90, bf16[1,2048,1024]{2,1,0:T(8,128)(2,1)} %param.29), kind=kOutput, calls=%fused_computation.13 | convolution fusion | flops 2150105088 | bytes 9437184 | tf_op jit(solution)/shard_map/dot_general | solution.py:116
  111.5 0.4 fusion.14
  111.9 0.4 convolution_bitcast_fusion.1
  112.3 59.7 %all-gather.3.cloned.1.call-done = bf16[64,24,2048]{2,1,0:T(8,128)(2,1)} async-done(((bf16[64,24,1024]{2,1,0:T(8,128)(2,1)}), bf16[64,24,2048]{2,1,0:T(8,128)(2,1)}) %all-gather.3.cloned.1.call-update) | async-done | bytes 6291472 | tf_op jit(solution)/shard_map/all_gather | solution.py:74
  172.0 12.3 %multiply_convert_fusion.1 = (bf16[1536,1024]{1,0:T(8,128)(2,1)S(1)}, f32[1536,1024]{1,0:T(8,128)}) fusion(bf16[1536,2048]{1,0:T(8,128)(2,1)} %bitcast.102, bf16[1,2048,1024]{2,1,0:T(8,128)(2,1)} %param.29), kind=kOutput, calls=%fused_computation.5 | convolution fusion | flops 6450315264 | bytes 19922944 | tf_op jit(solution)/shard_map/dot_general | solution.py:115
  184.3 0.9 fusion.13
  185.2 0.9 convolution_bitcast_fusion
  186.1 0.8 maximum_multiply_fusion
  187.2 31.6 %all-reduce.6.cloned.1.call-done = f32[19,2048]{1,0:T(8,128)} async-done(((f32[19,2048]{1,0:T(8,128)}), f32[19,2048]{1,0:T(8,128)}) %all-reduce.6.cloned.1.call-update) | async-done | bytes 155664 | tf_op jit(solution)/shard_map/psum | solution.py:130
  218.8 0.7 slice_reduce_fusion.1
  219.6 0.8 slice_reduce_fusion
  220.6 0.8 slice.63
  221.5 0.9 slice.62
  222.4 0.4 reshape.39
  223.9 4.8 while.17
  230.2 7.0 %multiply_convert_fusion = bf16[1536,1024]{1,0:T(8,128)(2,1)S(1)} fusion(f32[1536,1024]{1,0:T(8,128)} %get-tuple-element.150, f32[18,1536]{1,0:T(8,128)S(1)} %reshape.41, bf16[1024,18]{0,1:T(8,128)(2,1)S(1)} %copy-done, f32[1024]{0:T(1024)S(1)} %convert_element_type.54, f32[1536]{0:T(1024)S(1)} %mul.174), kind=kOutput, calls=%fused_computation.4 | convolution fusion | flops 357040128 | bytes 9594880 | tf_op jit(solution)/shard_map/ar,ha->rh/dot_general | solution.py:171
  237.2 9.2 %fusion.15 = f32[1024,2048]{1,0:T(8,128)S(1)} fusion(bf16[1536,1024]{1,0:T(8,128)(2,1)S(1)} %multiply_convert_fusion, bf16[1536,2048]{1,0:T(8,128)(2,1)} %bitcast.103), kind=kOutput, calls=%fused_computation.55 | convolution fusion | flops 6442450944 | bytes 17825792 | tf_op jit(solution)/shard_map/rd,rh->dh/dot_general | solution.py:179
  246.4 1.7 multiply_convert_fusion.2
  248.1 6.0 %add_bitcast_fusion = f32[1,2048,1024]{1,2,0:T(8,128)} fusion(f32[1024,2048]{1,0:T(8,128)S(1)} %fusion.15, bf16[512,1024]{1,0:T(8,128)(2,1)S(1)} %multiply_convert_fusion.2, bf16[512,2048]{1,0:T(8,128)(2,1)S(1)} %bitcast.91), kind=kOutput, calls=%fused_computation.3 | convolution fusion | flops 2149580800 | bytes 19922944 | tf_op jit(solution)/shard_map/rd,rh->dh/dot_general | solution.py:180
  254.2 291.0 %all-reduce.8.cloned.1.call-done = f32[1,2048,1024]{1,2,0:T(8,128)} async-done(((f32[1,2048,1024]{1,2,0:T(8,128)}), f32[1,2048,1024]{1,2,0:T(8,128)}) %all-reduce.8.cloned.1.call-update) | async-done | bytes 8388624 | tf_op jit(solution)/shard_map/psum | solution.py:183
  545.2 9.2 %copy.75 = f32[1,2048,1024]{2,1,0:T(8,128)} copy(f32[1,2048,1024]{1,2,0:T(8,128)} %all-reduce.8.cloned.1.call-done) | data formatting | bytes 16777216 | tf_op jit(solution)/shard_map/psum | solution.py:183
  (207 shorter events, 8.0 us)
Async XLA Ops:
  6.5 105.4 %copy-start = (bf16[1024,18]{0,1:T(8,128)(2,1)S(1)}, bf16[1024,18]{0,1:T(8,128)(2,1)}, u32[]{:S(2)}) copy-start(bf16[1024,18]{0,1:T(8,128)(2,1)} %param.31) | copy-start | bytes 110596
  11.8 77.0 %all-to-all-start.1 = ((bf16[16,96,1024]{2,0,1:T(8,128)(2,1)}), bf16[16,96,1024]{2,0,1:T(8,128)(2,1)S(1)}, u32[]{:S(2)}, u32[]{:S(2)}) async-start(bf16[16,96,1024]{2,0,1:T(8,128)(2,1)} %copy.65), calls=%async_computation.1 | async-start | bytes 6291456 | tf_op jit(solution)/shard_map/all_to_all | solution.py:109
  18.1 86.1 %all-gather.5.cloned.1.call-start = ((), (), s32[]{:S(2)}) async-start(), calls=%async_computation.3 | async-start | bytes 3145728 | tf_op jit(solution)/shard_map/all_gather | solution.py:75
  18.9 153.1 %all-gather.3.cloned.1.call-start = ((), (), s32[]{:S(2)}) async-start(), calls=%async_computation.2 | async-start | bytes 9437184 | tf_op jit(solution)/shard_map/all_gather | solution.py:74
  92.2 0.7 copy-start.3
  92.2 0.7 copy-start.4
  92.2 0.7 copy-start.5
  92.2 0.7 copy-start.6
  92.2 5.0 copy-start.11
  92.3 5.0 copy-start.12
  92.3 5.1 copy-start.2
  92.3 5.1 copy-start.7
  92.3 5.2 copy-start.8
  92.3 5.3 copy-start.9
  92.3 5.4 copy-start.10
  93.9 8.9 %all-to-all-start = ((f32[4,1,1536]{2,1,0:T(1,128)}), f32[4,1,1536]{2,1,0:T(1,128)S(1)}, u32[]{:S(2)}, u32[]{:S(2)}) async-start(f32[4,1,1536]{2,1,0:T(1,128)} %reshape.56), calls=%async_computation | async-start | bytes 49152 | tf_op jit(solution)/shard_map/all_to_all | solution.py:108
  97.2 121.6 %all-reduce.6.cloned.1.call-start = ((), (), s32[]{:S(2)}) async-start(), calls=%async_computation.4 | async-start | bytes 393216 | tf_op jit(solution)/shard_map/psum | solution.py:130
  186.9 358.3 %all-reduce.8.cloned.1.call-start = ((), (), s32[]{:S(2)}) async-start(), calls=%async_computation.5 | async-start | bytes 16777216 | tf_op jit(solution)/shard_map/psum | solution.py:183
  237.2 9.2 %copy-start.13 = (f32[512,1024]{1,0:T(8,128)S(1)}, f32[512,1024]{1,0:T(8,128)}, u32[]{:S(2)}) copy-start(f32[512,1024]{1,0:T(8,128)} %get-tuple-element.148) | copy-start | bytes 6291460
  246.4 1.7 copy-start.1
Sparse Core Ops, SparseCore 0:
  20.5 34.5 all-gather.4
  92.5 79.4 all-gather.2
  187.0 31.7 all-reduce.5
  254.3 290.8 all-reduce.7
where the time goes:
time: 562 us; the launch traced here: 561 us
  waiting for transfers between devices  458 us (81%)
  matrix products  46 us (8%)
  local copies, waits for them, and re-layouts  28.7 us (5%)
  between operations  13.5 us (2%)
  starting transfers between devices  9.88 us (2%)
    psum x1, waiting for transfers between devices, per_device(): summed = lax.psum(local_grad, 'dp')  291 us
    all_to_all x1, waiting for transfers between devices, per_device(): lax.all_to_all(online_obs, 'dp', split_axis=1, concat_axis=0, tiled=True)  69.9 us
    all_gather x1, waiting for transfers between devices, full_rows(): lax.all_gather(online_part, 'mp', axis=2, tiled=True)  59.7 us
    psum x1, waiting for transfers between devices, per_device(): heads = lax.psum(partial_value, ('mp', 'section'))  31.6 us
    dot_general x1, matrix products, per_device(): pre_online = jnp.dot(x_online, weight, preferred_element_type=jnp.float32)  12.3 us
  transfers between devices with their start and end apart: 6, of which 5 were waited for; matrix products, arithmetic and copies ran while one was open for 3% of the time, Pallas kernels for 0%

commit v1 on v0

--- a/solution.py
+++ b/solution.py
@@ -1,8 +1,11 @@
+import functools
 import math
 
 import jax
 import jax.numpy as jnp
 from jax import lax
+from jax.experimental import pallas as pl
+from jax.experimental.pallas import tpu as pltpu
 from jax.sharding import PartitionSpec as P
 
 DISCOUNT_RATE = 0.99
@@ -76,7 +79,7 @@
     )
 
 
-def per_device(
+def general_plan(
     online_obs,
     offline_obs,
     online_rewards,
@@ -184,7 +187,580 @@
     return summed[None]
 
 
+HEAD_ROWS = 24
+SPLIT_ROWS = 4 * HEAD_ROWS
+COLUMN_BLOCK = 256
+GRAD_CHUNKS = 8
+LANES = 128
+CODE_LIMIT = 32512.0
+CODE_TAIL = 16
+LOG_TWO = math.log(2.0)
+GRAD_LEAD = 3
+ONLINE_CHUNKS = 2
+VMEM_BYTES = 56 * 1024 * 1024
+SWAP = ((0, 1), (1, 0))
+TO_CENTER = ((0, 1), (3, 2))
+CENTER = ((1, 2), (2, 1))
+FROM_CENTER = ((1, 0), (2, 3))
+
+
+def params():
+    return pltpu.CompilerParams(vmem_limit_bytes=VMEM_BYTES)
+
+
+def cost(flops, nbytes, transcendentals=0):
+    return pl.CostEstimate(
+        flops=int(flops), bytes_accessed=int(nbytes), transcendentals=int(transcendentals)
+    )
+
+
+def whole(array):
+    rank = len(array.shape)
+    return pl.BlockSpec(array.shape, lambda *_: (0,) * rank)
+
+
+def untouched(arrays):
+    return [pl.BlockSpec(memory_space=pl.ANY) for _ in arrays]
+
+
+def forward_body(place, own_ref, other_ref, weight_ref, head_ref, slope_ref, heads_ref):
+    groups, width, features = own_ref.shape
+    m = place[0]
+    own_at = pl.multiple_of(m * features, features)
+    other_at = pl.multiple_of((1 - m) * features, features)
+    rows = groups * width
+    pre = jnp.dot(
+        own_ref[...].reshape(rows, features),
+        weight_ref[pl.ds(own_at, features), :],
+        preferred_element_type=jnp.float32,
+    )
+    pre = pre + jnp.dot(
+        other_ref[...].reshape(rows, features),
+        weight_ref[pl.ds(other_at, features), :],
+        preferred_element_type=jnp.float32,
+    )
+    sigma = 1.0 / (1.0 + jnp.exp(-pre))
+    slope_ref[...] = sigma * (1.0 + pre * (1.0 - sigma))
+    hidden = (pre * sigma).astype(jnp.bfloat16)
+
+    @pl.when(pl.program_id(0) == 0)
+    def _():
+        heads_ref[...] = jnp.zeros_like(heads_ref)
+
+    for g in range(groups):
+        part = lax.dot_general(
+            head_ref[...],
+            hidden[g * width : (g + 1) * width],
+            (((1,), (1,)), ((), ())),
+            preferred_element_type=jnp.float32,
+        )
+        heads_ref[g] += part[:HEAD_ROWS]
+
+
+def forward(place, own, first_group, other, weight, head):
+    groups, width, features = other.shape
+    hidden_count = weight.shape[1]
+    rows = groups * width
+    block = min(COLUMN_BLOCK, hidden_count)
+    at = first_group // groups
+    return pl.pallas_call(
+        forward_body,
+        grid_spec=pltpu.PrefetchScalarGridSpec(
+            num_scalar_prefetch=1,
+            grid=(hidden_count // block,),
+            in_specs=[
+                pl.BlockSpec((groups, width, features), lambda h, p: (at, 0, 0)),
+                pl.BlockSpec((groups, width, features), lambda h, p: (0, 0, 0)),
+                pl.BlockSpec((weight.shape[0], block), lambda h, p: (0, h)),
+                pl.BlockSpec((head.shape[0], block), lambda h, p: (0, h)),
+            ],
+            out_specs=[
+                pl.BlockSpec((rows, block), lambda h, p: (0, h)),
+                pl.BlockSpec((groups, HEAD_ROWS, width), lambda h, p: (0, 0, 0)),
+            ],
+        ),
+        out_shape=[
+            jax.ShapeDtypeStruct((rows, hidden_count), jnp.float32),
+            jax.ShapeDtypeStruct((groups, HEAD_ROWS, width), jnp.float32),
+        ],
+        compiler_params=params(),
+        cost_estimate=cost(
+            4 * rows * features * hidden_count,
+            8 * rows * hidden_count,
+            rows * hidden_count,
+        ),
+        name="forward_rows",
+    )(place, own, other, weight, head)
+
+
+def action_terms(parts, actions, behaviour, action_count):
+    heads = parts[0] + parts[1] + (parts[2] + parts[3])
+    row = lax.broadcasted_iota(jnp.int32, heads.shape, 0)
+    is_logit = row < action_count
+    logits = jnp.where(is_logit, heads, -1e30)
+    shifted = logits - jnp.max(logits, axis=0, keepdims=True)
+    log_sum = jnp.log(jnp.sum(jnp.exp(shifted), axis=0, keepdims=True))
+    log_probs = shifted - log_sum
+    taken = row == actions
+    chosen = jnp.sum(jnp.where(taken, log_probs, 0.0), axis=0, keepdims=True)
+    rho = jnp.exp(jnp.minimum(chosen - behaviour, 0.0))
+    spread = jnp.where(is_logit, jnp.exp(log_probs) - taken.astype(jnp.float32), 0.0)
+    return heads[action_count : action_count + 1], rho, spread
+
+
+def trace_terms(value, rho, reward, discount, length, position, axis, reach, scale):
+    size = value.shape[axis]
+    valid = (position < length).astype(jnp.float32)
+    valid_next = (position + 1 < length).astype(jnp.float32)
+    next_value = pltpu.roll(value, size - 1, axis) * valid_next
+    correction = valid * rho * (reward + discount * next_value - value)
+    coef = discount * TRACE_LAMBDA * rho * valid_next
+    shift = 1
+    while shift < reach:
+        correction = correction + coef * pltpu.roll(correction, size - shift, axis)
+        coef = coef * pltpu.roll(coef, size - shift, axis)
+        shift *= 2
+    targets = value + correction
+    next_target = pltpu.roll(targets, size - 1, axis) * valid_next
+    advantage = rho * (reward + discount * next_target - value)
+    return -scale * valid * correction, scale * (valid * advantage)
+
+
+def split_terms(logit_weight, value_weight, spread, action_count):
+    row = lax.broadcasted_iota(jnp.int32, spread.shape, 0)
+    full = jnp.where(row == action_count, value_weight, logit_weight * spread)
+    high = full.astype(jnp.bfloat16).astype(jnp.float32)
+    rest = full - high
+    middle = rest.astype(jnp.bfloat16).astype(jnp.float32)
+    low = rest - middle
+    return jnp.concatenate([high, middle, low, jnp.zeros_like(full)], axis=0).astype(jnp.bfloat16)
+
+
+def online_heads_body(action_count, *refs):
+    chunks = refs[: 4 * ONLINE_CHUNKS]
+    actions, behaviour, reward, done, pack_ref, spread_ref = refs[4 * ONLINE_CHUNKS :]
+    steps = actions.shape[0]
+    per_chunk = steps // ONLINE_CHUNKS
+    for t in range(steps):
+        c, g = divmod(t, per_chunk)
+        value, rho, spread = action_terms(
+            [chunks[4 * c + i][g] for i in range(4)],
+            actions[t : t + 1, :],
+            behaviour[t : t + 1, :],
+            action_count,
+        )
+        pack_ref[t : t + 1, :] = value
+        pack_ref[steps + t : steps + t + 1, :] = rho
+        spread_ref[t] = spread
+    pack_ref[2 * steps : 3 * steps, :] = reward[...]
+    pack_ref[3 * steps : 4 * steps, :] = DISCOUNT_RATE * (1.0 - done[...].astype(jnp.float32))
+
+
+def online_trace_body(action_count, scale, place, own, one, two, three, length, spread, terms_ref):
+    steps = spread.shape[0]
+    blocks = (own, one, two, three)
+
+    def field(i):
+        return jnp.concatenate([b[i * steps : (i + 1) * steps, :] for b in blocks], axis=0)
+
+    value = field(0)
+    position = lax.broadcasted_iota(jnp.int32, value.shape, 0) + place[2] * steps
+    value_weight, logit_weight = trace_terms(
+        value, field(1), field(2), field(3), length[...], position, 0, value.shape[0], scale
+    )
+    for t in range(steps):
+        terms_ref[t] = split_terms(
+            logit_weight[t : t + 1, :], value_weight[t : t + 1, :], spread[t], action_count
+        )
+
+
+def offline_trace_body(
+    action_count, step_count, scale, p0, p1, p2, p3, actions, behaviour, reward, done, length, terms_ref
+):
+    groups = terms_ref.shape[0]
+    values, rhos, spreads = [], [], []
+    for g in range(groups):
+        value, rho, spread = action_terms(
+            [p0[g], p1[g], p2[g], p3[g]],
+            actions[g : g + 1, :],
+            behaviour[g : g + 1, :],
+            action_count,
+        )
+        values.append(value)
+        rhos.append(rho)
+        spreads.append(spread)
+    value = jnp.concatenate(values, axis=0)
+    rho = jnp.concatenate(rhos, axis=0)
+    position = lax.rem(lax.broadcasted_iota(jnp.int32, value.shape, 1), step_count)
+    discount = DISCOUNT_RATE * (1.0 - done[...].astype(jnp.float32))
+    value_weight, logit_weight = trace_terms(
+        value, rho, reward[...], discount, length[...], position, 1, step_count, scale
+    )
+    for g in range(groups):
+        terms_ref[g] = split_terms(
+            logit_weight[g : g + 1, :], value_weight[g : g + 1, :], spreads[g], action_count
+        )
+
+
+def back_body(terms_ref, head_ref, slope_ref, dz_ref):
+    groups, _, width = terms_ref.shape
+    for g in range(groups):
+        rows = slice(g * width, (g + 1) * width)
+        dh = lax.dot_general(
+            terms_ref[g],
+            head_ref[...],
+            (((0,), (0,)), ((), ())),
+            preferred_element_type=jnp.float32,
+        )
+        dz_ref[rows, :] = (dh * slope_ref[rows, :]).astype(jnp.bfloat16)
+
+
+def back(terms, first_group, head, slope):
+    rows, hidden_count = slope.shape
+    width = terms.shape[2]
+    groups = rows // width
+    block = min(COLUMN_BLOCK, hidden_count)
+    at = first_group // groups
+    return pl.pallas_call(
+        back_body,
+        grid=(hidden_count // block,),
+        in_specs=[
+            pl.BlockSpec((groups, SPLIT_ROWS, width), lambda h: (at, 0, 0)),
+            pl.BlockSpec((SPLIT_ROWS, block), lambda h: (0, h)),
+            pl.BlockSpec((rows, block), lambda h: (0, h)),
+        ],
+        out_specs=pl.BlockSpec((rows, block), lambda h: (0, h)),
+        out_shape=jax.ShapeDtypeStruct((rows, hidden_count), jnp.bfloat16),
+        compiler_params=params(),
+        cost_estimate=cost(2 * rows * SPLIT_ROWS * hidden_count, 6 * rows * hidden_count),
+        name="back_rows",
+    )(terms, head, slope)
+
+
+def encode(blocks, message_ref):
+    rows = blocks[0].shape[0]
+    largest = functools.reduce(jnp.maximum, [jnp.abs(v) for v in blocks])
+    largest = jnp.max(jnp.max(largest, axis=0, keepdims=True), axis=1, keepdims=True)
+    exponent = jnp.ceil(jnp.log(jnp.maximum(largest, 1e-30)) * (1.0 / LOG_TWO) + 0.01)
+    scale = jnp.exp(exponent * -LOG_TWO) * CODE_LIMIT
+    for c, v in enumerate(blocks):
+        code = jnp.clip(jnp.floor(v * scale + 0.5), -CODE_LIMIT, CODE_LIMIT)
+        message_ref[c * rows : (c + 1) * rows, :] = code.astype(jnp.int32).astype(jnp.int16)
+    tail = jnp.broadcast_to(exponent, (CODE_TAIL, LANES)).astype(jnp.int32)
+    message_ref[len(blocks) * rows :, :] = tail.astype(jnp.int16)
+
+
+def decode(message_ref, count):
+    rows = (message_ref.shape[0] - CODE_TAIL) // count
+    exponent = message_ref[count * rows :, :].astype(jnp.int32).astype(jnp.float32)[:1, :]
+    step = jnp.exp(exponent * LOG_TWO) * (1.0 / CODE_LIMIT)
+    return [
+        message_ref[c * rows : (c + 1) * rows, :].astype(jnp.int32).astype(jnp.float32) * step
+        for c in range(count)
+    ]
+
+
+def message_shape(rows, columns):
+    return jax.ShapeDtypeStruct((rows * (columns // LANES) + CODE_TAIL, LANES), jnp.int16)
+
+
+def grad_body(count, deps, *refs):
+    xs, dzs = refs[:count], refs[count : 2 * count]
+    message_ref, sums_ref = refs[2 * count + deps :]
+    h = pl.program_id(0)
+    total = None
+    for x, dz in zip(xs, dzs):
+        part = lax.dot_general(
+            x[...], dz[...], (((0,), (0,)), ((), ())), preferred_element_type=jnp.float32
+        )
+        total = part if total is None else total + part
+    sums_ref[h] = total
+
+    @pl.when(h == pl.num_programs(0) - 1)
+    def _():
+        blocks = []
+        for i in range(sums_ref.shape[0]):
+            for c in range(sums_ref.shape[2] // LANES):
+                blocks.append(sums_ref[i, :, c * LANES : (c + 1) * LANES])
+        encode(blocks, message_ref)
+
+
+def grad_chunk(pieces, column, columns, deps):
+    hidden_count = pieces[0][2].shape[1]
+    block = min(COLUMN_BLOCK, hidden_count)
+    rows = sum(dz.shape[0] for _, _, dz in pieces)
+    message = message_shape(columns, hidden_count)
+
+    def x_spec(at, dz):
+        return pl.BlockSpec((dz.shape[0], columns), lambda h: (at, column))
+
+    return pl.pallas_call(
+        functools.partial(grad_body, len(pieces), len(deps)),
+        grid=(hidden_count // block,),
+        in_specs=[x_spec(at, dz) for _, at, dz in pieces]
+        + [pl.BlockSpec((dz.shape[0], block), lambda h: (0, h)) for _, _, dz in pieces]
+        + untouched(deps),
+        out_specs=whole(message),
+        out_shape=message,
+        scratch_shapes=[pltpu.VMEM((hidden_count // block, columns, block), jnp.float32)],
+        compiler_params=params(),
+        cost_estimate=cost(2 * rows * columns * hidden_count, 2 * rows * hidden_count),
+        name="grad_chunk",
+    )(*[x for x, _, _ in pieces], *[dz for _, _, dz in pieces], *deps)
+
+
+def add_body(count, a, b, *refs):
+    encode([u + v for u, v in zip(decode(a, count), decode(b, count))], refs[-1])
+
+
+def add_chunk(a, b, count, deps):
+    return pl.pallas_call(
+        functools.partial(add_body, count),
+        grid=(1,),
+        in_specs=[whole(a), whole(b)] + untouched(deps),
+        out_specs=whole(a),
+        out_shape=jax.ShapeDtypeStruct(a.shape, a.dtype),
+        compiler_params=params(),
+        cost_estimate=cost(a.size, 6 * a.size),
+        name="add_chunk",
+    )(a, b, *deps)
+
+
+def place_body(count, place, total, received, *refs):
+    out = refs[-1]
+    at_end = place[1] == 1
+
+    def write(message):
+        for c, v in enumerate(decode(message, count)):
+            out[:, c * LANES : (c + 1) * LANES] = v
+
+    @pl.when(at_end)
+    def _():
+        write(received)
+
+    @pl.when(jnp.logical_not(at_end))
+    def _():
+        write(total)
+
+
+def place_chunk(place, total, received, result, of_own, index, rows, shape, deps):
+    row_count, hidden_count = shape
+    per_half = row_count // (2 * rows)
+
+    def at(i, p):
+        half = p[0] if of_own else 1 - p[0]
+        return (half * per_half + index, 0)
+
+    earlier = [] if result is None else [result]
+    return pl.pallas_call(
+        functools.partial(place_body, hidden_count // LANES),
+        grid_spec=pltpu.PrefetchScalarGridSpec(
+            num_scalar_prefetch=1,
+            grid=(1,),
+            in_specs=[
+                pl.BlockSpec(total.shape, lambda i, p: (0, 0)),
+                pl.BlockSpec(total.shape, lambda i, p: (0, 0)),
+            ]
+            + untouched(earlier + deps),
+            out_specs=pl.BlockSpec((rows, hidden_count), at),
+        ),
+        out_shape=jax.ShapeDtypeStruct(shape, jnp.float32),
+        input_output_aliases={3: 0} if earlier else {},
+        compiler_params=params(),
+        cost_estimate=cost(total.size, 8 * total.size),
+        name="place_chunk",
+    )(place, total, received, *earlier, *deps)
+
+
+def other_half(obs, first, count, section):
+    half = count // 2
+    mine = lax.dynamic_slice_in_dim(obs, first + section * half, half, axis=0)
+    got = lax.ppermute(mine, "mp", SWAP)
+    rest = lax.ppermute(got, "section", SWAP)
+    return jnp.where(
+        section == 0,
+        jnp.concatenate([got, rest], axis=0),
+        jnp.concatenate([rest, got], axis=0),
+    )
+
+
+def from_chip_pair(part):
+    received = [part]
+    for flip in (1, 2, 3):
+        pairs = [(i, i ^ flip) for i in range(4)]
+        received.append(lax.ppermute(part, ("mp", "section"), pairs))
+    return received
+
+
+def line_plan(
+    online_obs,
+    offline_obs,
+    online_rewards,
+    offline_rewards,
+    online_behaviour,
+    offline_behaviour,
+    online_actions,
+    offline_actions,
+    online_done,
+    offline_done,
+    online_lengths,
+    offline_lengths,
+    torso_weights,
+    value_head,
+    policy_head,
+):
+    section = lax.axis_index("section")
+    m = lax.axis_index("mp")
+    z = lax.axis_index("dp")
+    dp = lax.axis_size("dp")
+    steps, online_count, features = online_obs.shape
+    offline_count, step_count, _ = offline_obs.shape
+    action_count = policy_head.shape[1]
+    hidden_count = value_head.shape[0]
+    place = jnp.stack([m, ((z == 0) | (z == dp - 1)).astype(jnp.int32), z]).astype(jnp.int32)
+    weight = torso_weights[0]
+    scale = math.sqrt(
+        hidden_count
+        * lax.axis_size("mp")
+        / ((online_count + offline_count * dp) * step_count)
+    )
+
+    offline_groups = offline_count // 2
+    offline_rows = offline_obs.reshape(offline_groups, 2 * step_count, features)
+    per_chunk = steps // ONLINE_CHUNKS
+    others = [
+        other_half(online_obs, c * per_chunk, per_chunk, section) for c in range(ONLINE_CHUNKS)
+    ]
+    other_offline = other_half(offline_rows, 0, offline_groups, section)
+
+    policy_rows = jnp.where(section == 1, policy_head.T, 0)
+    value_row = jnp.where(section == 0, value_head[None], 0)
+    head = jnp.concatenate([policy_rows, value_row], axis=0).astype(jnp.bfloat16)
+    head = jnp.pad(head, ((0, HEAD_ROWS - action_count - 1), (0, 0)))
+    forward_head = jnp.pad(head, ((0, 32 - HEAD_ROWS), (0, 0)))
+    back_head = jnp.concatenate([head, head, head, jnp.zeros_like(head)], axis=0)
+
+    owned = online_lengths.shape[0]
+    length_row = lax.dynamic_update_slice(
+        jnp.zeros((online_count,), jnp.float32), online_lengths.astype(jnp.float32), (z * owned,)
+    )
+    for flip in (1, 2):
+        length_row = length_row + lax.ppermute(
+            length_row, "dp", [(i, i ^ flip) for i in range(dp)]
+        )
+    length_row = length_row.astype(jnp.int32)[None]
+    lanes = (offline_groups, 2 * step_count)
+    offline_length = jnp.broadcast_to(
+        offline_lengths[:, None], (offline_count, step_count)
+    ).reshape(lanes)
+
+    slopes, online_parts = [], []
+    for c in range(ONLINE_CHUNKS):
+        slope, part = forward(
+            place, online_obs, c * per_chunk, others[c], weight, forward_head
+        )
+        slopes.append(slope)
+        online_parts += from_chip_pair(part)
+    offline_slope, offline_part = forward(
+        place, offline_rows, 0, other_offline, weight, forward_head
+    )
+    offline_parts = from_chip_pair(offline_part)
+
+    pack, spread = pl.pallas_call(
+        functools.partial(online_heads_body, action_count),
+        out_shape=[
+            jax.ShapeDtypeStruct((4 * steps, online_count), jnp.float32),
+            jax.ShapeDtypeStruct((steps, HEAD_ROWS, online_count), jnp.float32),
+        ],
+        compiler_params=params(),
+        name="online_heads",
+    )(*online_parts, online_actions, online_behaviour, online_rewards, online_done)
+    later = [
+        lax.ppermute(pack, "dp", [(i, i - hop) for i in range(hop, dp)]) for hop in range(1, dp)
+    ]
+    smem = pl.BlockSpec(memory_space=pltpu.SMEM)
+    vmem = pl.BlockSpec(memory_space=pltpu.VMEM)
+    online_terms = pl.pallas_call(
+        functools.partial(online_trace_body, action_count, scale),
+        in_specs=[smem] + [vmem] * 6,
+        out_specs=vmem,
+        out_shape=jax.ShapeDtypeStruct((steps, SPLIT_ROWS, online_count), jnp.bfloat16),
+        compiler_params=params(),
+        name="online_trace",
+    )(place, pack, *later, length_row, spread)
+    pieces = []
+    for c in range(ONLINE_CHUNKS):
+        pieces.append(back(online_terms, c * per_chunk, back_head, slopes[c]))
+
+    offline_terms = pl.pallas_call(
+        functools.partial(offline_trace_body, action_count, step_count, scale),
+        out_shape=jax.ShapeDtypeStruct(
+            (offline_groups, SPLIT_ROWS, 2 * step_count), jnp.bfloat16
+        ),
+        compiler_params=params(),
+        name="offline_trace",
+    )(
+        *offline_parts,
+        offline_actions.reshape(lanes),
+        offline_behaviour.reshape(lanes),
+        offline_rewards.reshape(lanes),
+        offline_done.reshape(lanes),
+        offline_length,
+    )
+    pieces.append(back(offline_terms, 0, back_head, offline_slope))
+
+    own_rows = online_obs.reshape(steps * online_count, features)
+    own_offline = offline_rows.reshape(-1, features)
+    own_x = [(own_rows, c) for c in range(ONLINE_CHUNKS)] + [(own_offline, 0)]
+    other_x = [(o.reshape(-1, features), 0) for o in others + [other_offline]]
+    columns = 2 * features // GRAD_CHUNKS
+    per_half = GRAD_CHUNKS // 2
+    lane_blocks = hidden_count // LANES
+
+    def local_grad(k, deps):
+        source = own_x if k < per_half else other_x
+        return grad_chunk(
+            [(x, at, dz) for (x, at), dz in zip(source, pieces)], k % per_half, columns, deps
+        )
+
+    inward, partial, across, total, outward = {}, {}, {}, {}, {}
+    own_grad = {}
+    result = None
+    for k in range(GRAD_LEAD):
+        own_grad[k] = local_grad(k, [])
+        inward[k] = lax.ppermute(own_grad[k], "dp", TO_CENTER)
+    for k in range(GRAD_CHUNKS + 2):
+        if k < GRAD_CHUNKS:
+            partial[k] = add_chunk(own_grad[k], inward[k], lane_blocks, [])
+            across[k] = lax.ppermute(partial[k], "dp", CENTER)
+        j = k - 1
+        if 0 <= j < GRAD_CHUNKS:
+            deps = [partial[k]] if k < GRAD_CHUNKS else []
+            total[j] = add_chunk(partial[j], across[j], lane_blocks, deps)
+            outward[j] = lax.ppermute(total[j], "dp", FROM_CENTER)
+            ahead = j + GRAD_LEAD
+            if ahead < GRAD_CHUNKS:
+                own_grad[ahead] = local_grad(ahead, [total[j]])
+                inward[ahead] = lax.ppermute(own_grad[ahead], "dp", TO_CENTER)
+        j = k - 2
+        if 0 <= j < GRAD_CHUNKS:
+            deps = [total[j + 1]] if j + 1 < GRAD_CHUNKS else []
+            result = place_chunk(
+                place,
+                total[j],
+                outward[j],
+                result,
+                j < per_half,
+                j % per_half,
+                columns,
+                (2 * features, hidden_count),
+                deps,
+            )
+    return result[None]
+
+
 def solution(mesh):
+    on_line = mesh.shape["dp"] == 4 and mesh.shape["mp"] == 2 and mesh.shape["section"] == 2
     in_specs = (
         P("dp", "groups", "mp"),
         P(("groups", "dp"), None, "mp"),
@@ -203,6 +779,7 @@
         P("mp", None),
     )
     out_specs = P(("groups", "section"), None, "mp")
+    per_device = line_plan if on_line else general_plan
     return jax.shard_map(
         per_device, mesh=mesh, in_specs=in_specs, out_specs=out_specs, check_vma=False
     )

time: 562 us -> 365 us (0.65)
  waiting for transfers between devices: 458 us -> 104 us
  Pallas kernels: 0 us -> 158 us
  starting transfers between devices: 9.88 us -> 68.4 us
  matrix products: 46 us -> 0 us
  between operations: 13.5 us -> 0.71 us
    psum x2 -> x0, waiting for transfers between devices: 323 us -> none  [the longest x1 291 us: per_device(): summed = lax.psum(local_grad, 'dp')]
    pallas_call x0 -> x41, Pallas kernels: none -> 158 us  [the longest x8 45.4 us: grad_chunk(): pl.pallas_call(functools.partial(grad_body, len(pieces), len(deps)), grid...]
    ppermute x0 -> x44, waiting for transfers between devices: none -> 104 us  [the longest x8 48.2 us: line_plan(): outward[j] = lax.ppermute(total[j], 'dp', FROM_CENTER)]
    all_to_all x2 -> x0, waiting for transfers between devices: 74.9 us -> none  [the longest x1 69.9 us: per_device(): lax.all_to_all(online_obs, 'dp', split_axis=1, concat_axis=0, tiled=True)]
    ppermute x0 -> x44, starting transfers between devices: none -> 68.4 us  [the longest x5 24.7 us: line_plan(): inward[ahead] = lax.ppermute(own_grad[ahead], 'dp', TO_CENTER)]
    all_gather x2 -> x0, waiting for transfers between devices: 59.7 us -> none  [the longest x1 59.7 us: full_rows(): lax.all_gather(online_part, 'mp', axis=2, tiled=True)]
    dot_general x10 -> x0, matrix products: 46 us -> none  [the longest x1 12.3 us: per_device(): pre_online = jnp.dot(x_online, weight, preferred_element_type=jnp.float32)]
    unnamed x36 -> x110, local copies, waits for them, and re-layouts: 7.28 us -> 17.6 us
  transfers between devices with their start and end apart: 6 -> 44, of which waited for: 5 -> 17; matrix products, arithmetic and copies ran while one was open for 3% -> 3% of each run, Pallas kernels for 0% -> 38%
where the time goes in v1:
time: 365 us; the launch traced here: 363 us
  Pallas kernels  158 us (43%)
  waiting for transfers between devices  104 us (28%)
  starting transfers between devices  68.4 us (19%)
  local copies, waits for them, and re-layouts  24.2 us (7%)
  other arithmetic  7.73 us (2%)
    ppermute x8, waiting for transfers between devices, line_plan(): outward[j] = lax.ppermute(total[j], 'dp', FROM_CENTER)  48.2 us
    pallas_call x8, Pallas kernels, grad_chunk(): pl.pallas_call(functools.partial(grad_body, len(pieces), len(deps)), grid...  45.4 us
    pallas_call x16, Pallas kernels, add_chunk(): pl.pallas_call(functools.partial(add_body, count), grid=(1,), in_specs=[w...  42.4 us
    ppermute x3, waiting for transfers between devices, other_half(): got = lax.ppermute(mine, 'mp', SWAP)  35 us
    pallas_call x3, Pallas kernels, forward(): pl.pallas_call(forward_body, grid_spec=pltpu.PrefetchScalarGridSpec(num_s...  27.3 us
    ppermute x5, starting transfers between devices, line_plan(): inward[ahead] = lax.ppermute(own_grad[ahead], 'dp', TO_CENTER)  24.7 us
    pallas_call x8, Pallas kernels, place_chunk(): pl.pallas_call(functools.partial(place_body, hidden_count // LANES), grid...  23.9 us
    unnamed x110, local copies, waits for them, and re-layouts  17.6 us
  transfers between devices with their start and end apart: 44, of which 17 were waited for; matrix products, arithmetic and copies ran while one was open for 3% of the time, Pallas kernels for 38%

profile of v1, /device:TPU:0, one launch (start us, length us, event | category | flops | bytes accessed | tf_op | source)
XLA Modules:
  0.0 363.2 jit_solution(16134772828610322487)
XLA Ops:
  1.7 3.0 collective-permute-start
  9.3 25.2 %collective-permute-done.4 = bf16[2,128,1024]{2,1,0:T(8,128)(2,1)} collective-permute-done((bf16[2,128,1024]{2,1,0:T(8,128)(2,1)}, bf16[2,128,1024]{2,1,0:T(8,128)(2,1)}, u32[]{:S(2)}, u32[]{:S(2)}) %collective-permute-start.4) | collective-permute-done | bytes 524320 | tf_op jit(solution)/shard_map/ppermute | solution.py:578
  40.5 9.8 %collective-permute-done.2 = bf16[4,96,1024]{2,1,0:T(8,128)(2,1)S(1)} collective-permute-done((bf16[4,96,1024]{2,1,0:T(8,128)(2,1)S(1)}, bf16[4,96,1024]{2,1,0:T(8,128)(2,1)S(1)}, u32[]{:S(2)}, u32[]{:S(2)}) %collective-permute-start.2) | collective-permute-done | bytes 786464 | tf_op jit(solution)/shard_map/ppermute | solution.py:578
  53.0 7.8 %forward_rows.5 = (f32[512,1024]{1,0:T(8,128)}, f32[4,24,128]{2,1,0:T(8,128)}) custom-call(s32[3]{0:T(128)} %pad_add_fusion.place, bf16[4,128,1024]{2,1,0:T(8,128)(2,1)} %bitcast.35, bf16[4,128,1024]{2,1,0:T(8,128)(2,1)} %maximum_select_fusion.2.other_ref, bf16[2048,1024]{1,0:T(8,128)(2,1)} %bitcast.41, bf16[32,1024]{1,0:T(8,128)(2,1)} %pad.9.head_ref), custom_call_target="tpu_custom_call" | custom-call | flops 2147483648 | bytes 4194304 | tf_op jit(solution)/shard_map/forward_rows/pallas_call | solution.py:266
  64.0 9.7 %forward_rows.3 = (f32[768,1024]{1,0:T(8,128)}, f32[8,24,96]{2,1,0:T(8,128)}) custom-call(s32[3]{0:T(128)} %pad_add_fusion.place, bf16[16,96,1024]{2,1,0:T(8,128)(2,1)} %own_ref.3, bf16[8,96,1024]{2,1,0:T(8,128)(2,1)} %maximum_select_fusion.other_ref, bf16[2048,1024]{1,0:T(8,128)(2,1)} %bitcast.42, bf16[32,1024]{1,0:T(8,128)(2,1)} %pad.9.head_ref), custom_call_target="tpu_custom_call" | custom-call | flops 3221225472 | bytes 6291456 | tf_op jit(solution)/shard_map/forward_rows/pallas_call | solution.py:266
  77.0 9.8 %forward_rows.4 = (f32[768,1024]{1,0:T(8,128)}, f32[8,24,96]{2,1,0:T(8,128)}) custom-call(s32[3]{0:T(128)} %pad_add_fusion.place, bf16[16,96,1024]{2,1,0:T(8,128)(2,1)} %own_ref.3, bf16[8,96,1024]{2,1,0:T(8,128)(2,1)} %maximum_select_fusion.1.other_ref, bf16[2048,1024]{1,0:T(8,128)(2,1)} %bitcast.43, bf16[32,1024]{1,0:T(8,128)(2,1)} %pad.9.head_ref), custom_call_target="tpu_custom_call" | custom-call | flops 3221225472 | bytes 6291456 | tf_op jit(solution)/shard_map/forward_rows/pallas_call | solution.py:266
  105.6 4.2 %back_rows.5.refs_5_ = bf16[512,1024]{1,0:T(8,128)(2,1)} custom-call(bf16[4,96,128]{2,1,0:T(8,128)(2,1)} %offline_trace.1.terms_ref, bf16[96,1024]{1,0:T(8,128)(2,1)} %maximum_maximum_fusion.head_ref, f32[512,1024]{1,0:T(8,128)} %get-tuple-element.20.slope_ref), custom_call_target="tpu_custom_call" | custom-call | flops 100663296 | bytes 3145728 | tf_op jit(solution)/shard_map/back_rows/pallas_call | solution.py:424
  112.3 4.6 %back_rows.4.refs_4_ = bf16[768,1024]{1,0:T(8,128)(2,1)} custom-call(bf16[16,96,96]{2,1,0:T(8,128)(2,1)} %online_trace.1.terms_ref, bf16[96,1024]{1,0:T(8,128)(2,1)} %maximum_maximum_fusion.head_ref, f32[768,1024]{1,0:T(8,128)} %get-tuple-element.18.slope_ref), custom_call_target="tpu_custom_call" | custom-call | flops 150994944 | bytes 4718592 | tf_op jit(solution)/shard_map/back_rows/pallas_call | solution.py:424
  116.9 4.6 %back_rows.3.refs_3_ = bf16[768,1024]{1,0:T(8,128)(2,1)} custom-call(bf16[16,96,96]{2,1,0:T(8,128)(2,1)} %online_trace.1.terms_ref, bf16[96,1024]{1,0:T(8,128)(2,1)} %maximum_maximum_fusion.head_ref, f32[768,1024]{1,0:T(8,128)} %get-tuple-element.17.slope_ref), custom_call_target="tpu_custom_call" | custom-call | flops 150994944 | bytes 4718592 | tf_op jit(solution)/shard_map/back_rows/pallas_call | solution.py:424
  121.5 5.7 %grad_chunk.11.a = s16[2064,128]{1,0:T(8,128)(2,1)} custom-call(bf16[1536,1024]{1,0:T(8,128)(2,1)} %bitcast.15, bf16[1536,1024]{1,0:T(8,128)(2,1)} %bitcast.16, bf16[512,1024]{1,0:T(8,128)(2,1)} %bitcast.36, bf16[768,1024]{1,0:T(8,128)(2,1)} %back_rows.3.refs_3_, bf16[768,1024]{1,0:T(8,128)(2,1)} %back_rows.4.refs_4_, bf16[512,1024]{1,0:T(8,128)(2,1)} %back_rows.5.refs_5_), custom_call_target="tpu_custom_call" | custom-call | flops 1073741824 | bytes 4194304 | tf_op jit(solution)/shard_map/grad_chunk/pallas_call | solution.py:497
  127.2 4.6 %collective-permute-start.26 = (s16[2064,128]{1,0:T(8,128)(2,1)}, s16[2064,128]{1,0:T(8,128)(2,1)S(1)}, u32[]{:S(2)}, u32[]{:S(2)}) collective-permute-start(s16[2064,128]{1,0:T(8,128)(2,1)} %grad_chunk.11.a), channel_id=1, source_target_pairs={{0,4},{12,8},{1,5},{13,9},{2,6},{14,10},{3,7},{15,11},{16,20},{28,... | collective-permute-start | bytes 1585160 | tf_op jit(solution)/shard_map/ppermute | solution.py:731
  131.8 5.7 %grad_chunk.8.a = s16[2064,128]{1,0:T(8,128)(2,1)} custom-call(bf16[1536,1024]{1,0:T(8,128)(2,1)} %bitcast.17, bf16[1536,1024]{1,0:T(8,128)(2,1)} %bitcast.18, bf16[512,1024]{1,0:T(8,128)(2,1)} %bitcast.37, bf16[768,1024]{1,0:T(8,128)(2,1)} %back_rows.3.refs_3_, bf16[768,1024]{1,0:T(8,128)(2,1)} %back_rows.4.refs_4_, bf16[512,1024]{1,0:T(8,128)(2,1)} %back_rows.5.refs_5_), custom_call_target="tpu_custom_call" | custom-call | flops 1073741824 | bytes 4194304 | tf_op jit(solution)/shard_map/grad_chunk/pallas_call | solution.py:497
  138.8 5.7 %grad_chunk.9.a = s16[2064,128]{1,0:T(8,128)(2,1)} custom-call(bf16[1536,1024]{1,0:T(8,128)(2,1)} %bitcast.19, bf16[1536,1024]{1,0:T(8,128)(2,1)} %bitcast.20, bf16[512,1024]{1,0:T(8,128)(2,1)} %bitcast.38, bf16[768,1024]{1,0:T(8,128)(2,1)} %back_rows.3.refs_3_, bf16[768,1024]{1,0:T(8,128)(2,1)} %back_rows.4.refs_4_, bf16[512,1024]{1,0:T(8,128)(2,1)} %back_rows.5.refs_5_), custom_call_target="tpu_custom_call" | custom-call | flops 1073741824 | bytes 4194304 | tf_op jit(solution)/shard_map/grad_chunk/pallas_call | solution.py:497
  149.9 5.9 %collective-permute-done.20.b = s16[2064,128]{1,0:T(8,128)(2,1)S(1)} collective-permute-done((s16[2064,128]{1,0:T(8,128)(2,1)}, s16[2064,128]{1,0:T(8,128)(2,1)S(1)}, u32[]{:S(2)}, u32[]{:S(2)}) %collective-permute-start.20) | collective-permute-done | bytes 528416 | tf_op jit(solution)/shard_map/ppermute | solution.py:731
  160.1 5.6 %collective-permute-done.22.b = s16[2064,128]{1,0:T(8,128)(2,1)S(1)} collective-permute-done((s16[2064,128]{1,0:T(8,128)(2,1)}, s16[2064,128]{1,0:T(8,128)(2,1)S(1)}, u32[]{:S(2)}, u32[]{:S(2)}) %collective-permute-start.22) | collective-permute-done | bytes 528416 | tf_op jit(solution)/shard_map/ppermute | solution.py:731
  173.3 5.7 %grad_chunk.12.a = s16[2064,128]{1,0:T(8,128)(2,1)} custom-call(bf16[1536,1024]{1,0:T(8,128)(2,1)} %bitcast.21, bf16[1536,1024]{1,0:T(8,128)(2,1)} %bitcast.22, bf16[512,1024]{1,0:T(8,128)(2,1)} %bitcast.39, bf16[768,1024]{1,0:T(8,128)(2,1)} %back_rows.3.refs_3_, bf16[768,1024]{1,0:T(8,128)(2,1)} %back_rows.4.refs_4_, bf16[512,1024]{1,0:T(8,128)(2,1)} %back_rows.5.refs_5_, ...), custom_call_target="tpu_custom_call" | custom-call | flops 1073741824 | bytes 4194304 | tf_op jit(solution)/shard_map/grad_chunk/pallas_call | solution.py:497
  179.0 7.6 %collective-permute-start.28 = (s16[2064,128]{1,0:T(8,128)(2,1)}, s16[2064,128]{1,0:T(8,128)(2,1)S(1)}, u32[]{:S(2)}, u32[]{:S(2)}) collective-permute-start(s16[2064,128]{1,0:T(8,128)(2,1)} %grad_chunk.12.a), channel_id=1, source_target_pairs={{0,4},{12,8},{1,5},{13,9},{2,6},{14,10},{3,7},{15,11},{16,20},{28,... | collective-permute-start | bytes 1585160 | tf_op jit(solution)/shard_map/ppermute | solution.py:744
  190.1 5.7 %grad_chunk.10.a = s16[2064,128]{1,0:T(8,128)(2,1)} custom-call(bf16[768,1024]{1,0:T(8,128)(2,1)} %bitcast.23, bf16[768,1024]{1,0:T(8,128)(2,1)} %bitcast.27, bf16[512,1024]{1,0:T(8,128)(2,1)} %bitcast.31, bf16[768,1024]{1,0:T(8,128)(2,1)} %back_rows.3.refs_3_, bf16[768,1024]{1,0:T(8,128)(2,1)} %back_rows.4.refs_4_, bf16[512,1024]{1,0:T(8,128)(2,1)} %back_rows.5.refs_5_, ...), custom_call_target="tpu_custom_call" | custom-call | flops 1073741824 | bytes 4194304 | tf_op jit(solution)/shard_map/grad_chunk/pallas_call | solution.py:497
  204.5 5.7 %grad_chunk.13.a = s16[2064,128]{1,0:T(8,128)(2,1)} custom-call(bf16[768,1024]{1,0:T(8,128)(2,1)} %bitcast.24, bf16[768,1024]{1,0:T(8,128)(2,1)} %bitcast.28, bf16[512,1024]{1,0:T(8,128)(2,1)} %bitcast.32, bf16[768,1024]{1,0:T(8,128)(2,1)} %back_rows.3.refs_3_, bf16[768,1024]{1,0:T(8,128)(2,1)} %back_rows.4.refs_4_, bf16[512,1024]{1,0:T(8,128)(2,1)} %back_rows.5.refs_5_, ...), custom_call_target="tpu_custom_call" | custom-call | flops 1073741824 | bytes 4194304 | tf_op jit(solution)/shard_map/grad_chunk/pallas_call | solution.py:497
  210.1 4.4 %collective-permute-start.29 = (s16[2064,128]{1,0:T(8,128)(2,1)}, s16[2064,128]{1,0:T(8,128)(2,1)S(1)}, u32[]{:S(2)}, u32[]{:S(2)}) collective-permute-start(s16[2064,128]{1,0:T(8,128)(2,1)} %grad_chunk.13.a), channel_id=1, source_target_pairs={{0,4},{12,8},{1,5},{13,9},{2,6},{14,10},{3,7},{15,11},{16,20},{28,... | collective-permute-start | bytes 1585160 | tf_op jit(solution)/shard_map/ppermute | solution.py:744
  219.4 3.5 collective-permute-done.29.b
  229.9 5.7 %grad_chunk.14.a = s16[2064,128]{1,0:T(8,128)(2,1)} custom-call(bf16[768,1024]{1,0:T(8,128)(2,1)} %bitcast.25, bf16[768,1024]{1,0:T(8,128)(2,1)} %bitcast.29, bf16[512,1024]{1,0:T(8,128)(2,1)} %bitcast.33, bf16[768,1024]{1,0:T(8,128)(2,1)} %back_rows.3.refs_3_, bf16[768,1024]{1,0:T(8,128)(2,1)} %back_rows.4.refs_4_, bf16[512,1024]{1,0:T(8,128)(2,1)} %back_rows.5.refs_5_, ...), custom_call_target="tpu_custom_call" | custom-call | flops 1073741824 | bytes 4194304 | tf_op jit(solution)/shard_map/grad_chunk/pallas_call | solution.py:497
  235.5 9.9 %collective-permute-start.30 = (s16[2064,128]{1,0:T(8,128)(2,1)}, s16[2064,128]{1,0:T(8,128)(2,1)S(1)}, u32[]{:S(2)}, u32[]{:S(2)}) collective-permute-start(s16[2064,128]{1,0:T(8,128)(2,1)} %grad_chunk.14.a), channel_id=1, source_target_pairs={{0,4},{12,8},{1,5},{13,9},{2,6},{14,10},{3,7},{15,11},{16,20},{28,... | collective-permute-start | bytes 1585160 | tf_op jit(solution)/shard_map/ppermute | solution.py:744
  248.9 5.7 %grad_chunk.15.a = s16[2064,128]{1,0:T(8,128)(2,1)} custom-call(bf16[768,1024]{1,0:T(8,128)(2,1)} %bitcast.26, bf16[768,1024]{1,0:T(8,128)(2,1)} %bitcast.30, bf16[512,1024]{1,0:T(8,128)(2,1)} %bitcast.34, bf16[768,1024]{1,0:T(8,128)(2,1)} %back_rows.3.refs_3_, bf16[768,1024]{1,0:T(8,128)(2,1)} %back_rows.4.refs_4_, bf16[512,1024]{1,0:T(8,128)(2,1)} %back_rows.5.refs_5_, ...), custom_call_target="tpu_custom_call" | custom-call | flops 1073741824 | bytes 4194304 | tf_op jit(solution)/shard_map/grad_chunk/pallas_call | solution.py:497
  283.1 3.0 collective-permute-done.42.received
  287.4 10.0 %collective-permute-done.43.received = s16[2064,128]{1,0:T(8,128)(2,1)S(1)} collective-permute-done((s16[2064,128]{1,0:T(8,128)(2,1)S(1)}, s16[2064,128]{1,0:T(8,128)(2,1)S(1)}, u32[]{:S(2)}, u32[]{:S(2)}) %collective-permute-start.43) | collective-permute-done | bytes 528416 | tf_op jit(solution)/shard_map/ppermute | solution.py:740
  298.7 10.0 %collective-permute-done.41.received = s16[2064,128]{1,0:T(8,128)(2,1)S(1)} collective-permute-done((s16[2064,128]{1,0:T(8,128)(2,1)S(1)}, s16[2064,128]{1,0:T(8,128)(2,1)S(1)}, u32[]{:S(2)}, u32[]{:S(2)}) %collective-permute-start.41) | collective-permute-done | bytes 528416 | tf_op jit(solution)/shard_map/ppermute | solution.py:740
  310.1 3.0 place_chunk.8.refs_0_
  313.1 3.0 place_chunk.9.refs_0_
  323.9 7.5 %collective-permute-done.39.received = s16[2064,128]{1,0:T(8,128)(2,1)S(1)} collective-permute-done((s16[2064,128]{1,0:T(8,128)(2,1)S(1)}, s16[2064,128]{1,0:T(8,128)(2,1)S(1)}, u32[]{:S(2)}, u32[]{:S(2)}) %collective-permute-start.39) | collective-permute-done | bytes 528416 | tf_op jit(solution)/shard_map/ppermute | solution.py:740
  335.2 7.5 %collective-permute-done.38.received = s16[2064,128]{1,0:T(8,128)(2,1)S(1)} collective-permute-done((s16[2064,128]{1,0:T(8,128)(2,1)S(1)}, s16[2064,128]{1,0:T(8,128)(2,1)S(1)}, u32[]{:S(2)}, u32[]{:S(2)}) %collective-permute-start.38) | collective-permute-done | bytes 528416 | tf_op jit(solution)/shard_map/ppermute | solution.py:740
  346.6 7.2 %collective-permute-done.36.received = s16[2064,128]{1,0:T(8,128)(2,1)S(1)} collective-permute-done((s16[2064,128]{1,0:T(8,128)(2,1)}, s16[2064,128]{1,0:T(8,128)(2,1)S(1)}, u32[]{:S(2)}, u32[]{:S(2)}) %collective-permute-start.36) | collective-permute-done | bytes 528416 | tf_op jit(solution)/shard_map/ppermute | solution.py:740
  (232 shorter events, 145.7 us)
Async XLA Ops:
  1.7 36.2 %collective-permute-start = (bf16[4,96,1024]{2,1,0:T(8,128)(2,1)S(1)}, bf16[4,96,1024]{2,1,0:T(8,128)(2,1)S(1)}, u32[]{:S(2)}, u32[]{:S(2)}) collective-permute-start(bf16[4,96,1024]{2,1,0:T(8,128)(2,1)S(1)} %get-tuple-element.22), channel_id=1, source_target_pairs={{0,2},{2,0},{1,3},{3,1},{4,6},{6,4},{5,7},{7,5},{8,10},{10,8},{9,1... | collective-permute-start | bytes 2359304 | tf_op jit(solution)/shard_map/ppermute | solution.py:578
  5.5 28.9 %collective-permute-start.4 = (bf16[2,128,1024]{2,1,0:T(8,128)(2,1)}, bf16[2,128,1024]{2,1,0:T(8,128)(2,1)}, u32[]{:S(2)}, u32[]{:S(2)}) collective-permute-start(bf16[2,128,1024]{2,1,0:T(8,128)(2,1)} %constant_dynamic-slice_fusion), channel_id=1, source_target_pairs={{0,2},{2,0},{1,3},{3,1},{4,6},{6,4},{5,7},{7,5},{8,10},{10,8},{9,1... | collective-permute-start | bytes 1572872 | tf_op jit(solution)/shard_map/ppermute | solution.py:578
  5.7 81.1 %collective-permute-start.15 = (f32[96]{0:T(128)S(1)}, f32[96]{0:T(128)S(1)}, u32[]{:S(2)}, u32[]{:S(2)}) collective-permute-start(f32[96]{0:T(128)S(1)} %convert_dynamic-update-slice_fusion), channel_id=1, source_target_pairs={{0,4},{4,0},{8,12},{12,8},{1,5},{5,1},{9,13},{13,9},{2,6},{6,2},{1... | collective-permute-start | bytes 1160 | tf_op jit(solution)/shard_map/ppermute | solution.py:648
  7.8 42.6 %collective-permute-start.2 = (bf16[4,96,1024]{2,1,0:T(8,128)(2,1)S(1)}, bf16[4,96,1024]{2,1,0:T(8,128)(2,1)S(1)}, u32[]{:S(2)}, u32[]{:S(2)}) collective-permute-start(bf16[4,96,1024]{2,1,0:T(8,128)(2,1)S(1)} %get-tuple-element.21), channel_id=1, source_target_pairs={{0,2},{2,0},{1,3},{3,1},{4,6},{6,4},{5,7},{7,5},{8,10},{10,8},{9,1... | collective-permute-start | bytes 2359304 | tf_op jit(solution)/shard_map/ppermute | solution.py:578
  34.4 15.9 %collective-permute-start.5 = (bf16[2,128,1024]{2,1,0:T(8,128)(2,1)}, bf16[2,128,1024]{2,1,0:T(8,128)(2,1)}, u32[]{:S(2)}, u32[]{:S(2)}) collective-permute-start(bf16[2,128,1024]{2,1,0:T(8,128)(2,1)} %collective-permute-done.4), channel_id=1, source_target_pairs={{0,1},{1,0},{2,3},{3,2},{4,5},{5,4},{6,7},{7,6},{8,9},{9,8},{10,11... | collective-permute-start | bytes 1572872 | tf_op jit(solution)/shard_map/ppermute | solution.py:579
  37.9 24.8 %collective-permute-start.1 = (bf16[4,96,1024]{2,1,0:T(8,128)(2,1)S(1)}, bf16[4,96,1024]{2,1,0:T(8,128)(2,1)S(1)}, u32[]{:S(2)}, u32[]{:S(2)}) collective-permute-start(bf16[4,96,1024]{2,1,0:T(8,128)(2,1)S(1)} %collective-permute-done), channel_id=1, source_target_pairs={{0,1},{1,0},{2,3},{3,2},{4,5},{5,4},{6,7},{7,6},{8,9},{9,8},{10,11... | collective-permute-start | bytes 2359304 | tf_op jit(solution)/shard_map/ppermute | solution.py:579
  50.3 25.0 %collective-permute-start.3 = (bf16[4,96,1024]{2,1,0:T(8,128)(2,1)S(1)}, bf16[4,96,1024]{2,1,0:T(8,128)(2,1)S(1)}, u32[]{:S(2)}, u32[]{:S(2)}) collective-permute-start(bf16[4,96,1024]{2,1,0:T(8,128)(2,1)S(1)} %collective-permute-done.2), channel_id=1, source_target_pairs={{0,1},{1,0},{2,3},{3,2},{4,5},{5,4},{6,7},{7,6},{8,9},{9,8},{10,11... | collective-permute-start | bytes 2359304 | tf_op jit(solution)/shard_map/ppermute | solution.py:579
  60.8 39.5 %collective-permute-start.19 = (f32[4,24,128]{2,1,0:T(8,128)}, f32[4,24,128]{2,1,0:T(8,128)S(1)}, u32[]{:S(2)}, u32[]{:S(2)}) collective-permute-start(f32[4,24,128]{2,1,0:T(8,128)} %get-tuple-element.19.p0), channel_id=1, source_target_pairs={{0,3},{1,2},{2,1},{3,0},{4,7},{5,6},{6,5},{7,4},{8,11},{9,10},{10,... | collective-permute-start | bytes 147464 | tf_op jit(solution)/shard_map/ppermute | solution.py:591
  73.7 13.6 %collective-permute-start.8 = (f32[8,24,96]{2,1,0:T(8,128)}, f32[8,24,96]{2,1,0:T(8,128)S(1)}, u32[]{:S(2)}, u32[]{:S(2)}) collective-permute-start(f32[8,24,96]{2,1,0:T(8,128)} %get-tuple-element.13.refs_0_), channel_id=1, source_target_pairs={{0,3},{1,2},{2,1},{3,0},{4,7},{5,6},{6,5},{7,4},{8,11},{9,10},{10,... | collective-permute-start | bytes 221192 | tf_op jit(solution)/shard_map/ppermute | solution.py:591
  73.7 15.1 %collective-permute-start.7 = (f32[8,24,96]{2,1,0:T(8,128)}, f32[8,24,96]{2,1,0:T(8,128)S(1)}, u32[]{:S(2)}, u32[]{:S(2)}) collective-permute-start(f32[8,24,96]{2,1,0:T(8,128)} %get-tuple-element.13.refs_0_), channel_id=1, source_target_pairs={{0,2},{1,3},{2,0},{3,1},{4,6},{5,7},{6,4},{7,5},{8,10},{9,11},{10,... | collective-permute-start | bytes 221192 | tf_op jit(solution)/shard_map/ppermute | solution.py:591
  75.3 13.7 %collective-permute-start.6 = (f32[8,24,96]{2,1,0:T(8,128)}, f32[8,24,96]{2,1,0:T(8,128)S(1)}, u32[]{:S(2)}, u32[]{:S(2)}) collective-permute-start(f32[8,24,96]{2,1,0:T(8,128)} %get-tuple-element.13.refs_0_), channel_id=1, source_target_pairs={{0,1},{1,0},{2,3},{3,2},{4,5},{5,4},{6,7},{7,6},{8,9},{9,8},{10,11... | collective-permute-start | bytes 221192 | tf_op jit(solution)/shard_map/ppermute | solution.py:591
  127.2 18.6 %collective-permute-start.26 = (s16[2064,128]{1,0:T(8,128)(2,1)}, s16[2064,128]{1,0:T(8,128)(2,1)S(1)}, u32[]{:S(2)}, u32[]{:S(2)}) collective-permute-start(s16[2064,128]{1,0:T(8,128)(2,1)} %grad_chunk.11.a), channel_id=1, source_target_pairs={{0,4},{12,8},{1,5},{13,9},{2,6},{14,10},{3,7},{15,11},{16,20},{28,... | collective-permute-start | bytes 1585160 | tf_op jit(solution)/shard_map/ppermute | solution.py:731
  137.4 18.4 %collective-permute-start.20 = (s16[2064,128]{1,0:T(8,128)(2,1)}, s16[2064,128]{1,0:T(8,128)(2,1)S(1)}, u32[]{:S(2)}, u32[]{:S(2)}) collective-permute-start(s16[2064,128]{1,0:T(8,128)(2,1)} %grad_chunk.8.a), channel_id=1, source_target_pairs={{0,4},{12,8},{1,5},{13,9},{2,6},{14,10},{3,7},{15,11},{16,20},{28,... | collective-permute-start | bytes 1585160 | tf_op jit(solution)/shard_map/ppermute | solution.py:731
  144.4 21.3 %collective-permute-start.22 = (s16[2064,128]{1,0:T(8,128)(2,1)}, s16[2064,128]{1,0:T(8,128)(2,1)S(1)}, u32[]{:S(2)}, u32[]{:S(2)}) collective-permute-start(s16[2064,128]{1,0:T(8,128)(2,1)} %grad_chunk.9.a), channel_id=1, source_target_pairs={{0,4},{12,8},{1,5},{13,9},{2,6},{14,10},{3,7},{15,11},{16,20},{28,... | collective-permute-start | bytes 1585160 | tf_op jit(solution)/shard_map/ppermute | solution.py:731
  149.2 20.6 %collective-permute-start.27 = (s16[2064,128]{1,0:T(8,128)(2,1)}, s16[2064,128]{1,0:T(8,128)(2,1)S(1)}, u32[]{:S(2)}, u32[]{:S(2)}) collective-permute-start(s16[2064,128]{1,0:T(8,128)(2,1)} %add_chunk.20.a), channel_id=1, source_target_pairs={{4,8},{8,4},{5,9},{9,5},{6,10},{10,6},{7,11},{11,7},{20,24},{24,20... | collective-permute-start | bytes 1585160 | tf_op jit(solution)/shard_map/ppermute | solution.py:735
  159.2 27.4 %collective-permute-start.21 = (s16[2064,128]{1,0:T(8,128)(2,1)}, s16[2064,128]{1,0:T(8,128)(2,1)S(1)}, u32[]{:S(2)}, u32[]{:S(2)}) collective-permute-start(s16[2064,128]{1,0:T(8,128)(2,1)} %add_chunk.16.a.refs_0_), channel_id=1, source_target_pairs={{4,8},{8,4},{5,9},{9,5},{6,10},{10,6},{7,11},{11,7},{20,24},{24,20... | collective-permute-start | bytes 1585160 | tf_op jit(solution)/shard_map/ppermute | solution.py:735
  169.2 31.8 %collective-permute-start.25 = (s16[2064,128]{1,0:T(8,128)(2,1)}, s16[2064,128]{1,0:T(8,128)(2,1)S(1)}, u32[]{:S(2)}, u32[]{:S(2)}) collective-permute-start(s16[2064,128]{1,0:T(8,128)(2,1)} %add_chunk.17.refs_0_.a), channel_id=1, source_target_pairs={{4,8},{8,4},{5,9},{9,5},{6,10},{10,6},{7,11},{11,7},{20,24},{24,20... | collective-permute-start | bytes 1585160 | tf_op jit(solution)/shard_map/ppermute | solution.py:735
  179.0 18.5 %collective-permute-start.28 = (s16[2064,128]{1,0:T(8,128)(2,1)}, s16[2064,128]{1,0:T(8,128)(2,1)S(1)}, u32[]{:S(2)}, u32[]{:S(2)}) collective-permute-start(s16[2064,128]{1,0:T(8,128)(2,1)} %grad_chunk.12.a), channel_id=1, source_target_pairs={{0,4},{12,8},{1,5},{13,9},{2,6},{14,10},{3,7},{15,11},{16,20},{28,... | collective-permute-start | bytes 1585160 | tf_op jit(solution)/shard_map/ppermute | solution.py:744
  195.7 18.8 %collective-permute-start.23 = (s16[2064,128]{1,0:T(8,128)(2,1)}, s16[2064,128]{1,0:T(8,128)(2,1)S(1)}, u32[]{:S(2)}, u32[]{:S(2)}) collective-permute-start(s16[2064,128]{1,0:T(8,128)(2,1)} %grad_chunk.10.a), channel_id=1, source_target_pairs={{0,4},{12,8},{1,5},{13,9},{2,6},{14,10},{3,7},{15,11},{16,20},{28,... | collective-permute-start | bytes 1585160 | tf_op jit(solution)/shard_map/ppermute | solution.py:744
  210.1 12.9 %collective-permute-start.29 = (s16[2064,128]{1,0:T(8,128)(2,1)}, s16[2064,128]{1,0:T(8,128)(2,1)S(1)}, u32[]{:S(2)}, u32[]{:S(2)}) collective-permute-start(s16[2064,128]{1,0:T(8,128)(2,1)} %grad_chunk.13.a), channel_id=1, source_target_pairs={{0,4},{12,8},{1,5},{13,9},{2,6},{14,10},{3,7},{15,11},{16,20},{28,... | collective-permute-start | bytes 1585160 | tf_op jit(solution)/shard_map/ppermute | solution.py:744
  218.7 26.7 %collective-permute-start.33 = (s16[2064,128]{1,0:T(8,128)(2,1)S(1)}, s16[2064,128]{1,0:T(8,128)(2,1)S(1)}, u32[]{:S(2)}, u32[]{:S(2)}) collective-permute-start(s16[2064,128]{1,0:T(8,128)(2,1)S(1)} %copy-done.7), channel_id=1, source_target_pairs={{4,8},{8,4},{5,9},{9,5},{6,10},{10,6},{7,11},{11,7},{20,24},{24,20... | collective-permute-start | bytes 1585160 | tf_op jit(solution)/shard_map/ppermute | solution.py:735
  235.5 21.3 %collective-permute-start.30 = (s16[2064,128]{1,0:T(8,128)(2,1)}, s16[2064,128]{1,0:T(8,128)(2,1)S(1)}, u32[]{:S(2)}, u32[]{:S(2)}) collective-permute-start(s16[2064,128]{1,0:T(8,128)(2,1)} %grad_chunk.14.a), channel_id=1, source_target_pairs={{0,4},{12,8},{1,5},{13,9},{2,6},{14,10},{3,7},{15,11},{16,20},{28,... | collective-permute-start | bytes 1585160 | tf_op jit(solution)/shard_map/ppermute | solution.py:744
  256.1 14.8 %collective-permute-start.37 = (s16[2064,128]{1,0:T(8,128)(2,1)S(1)}, s16[2064,128]{1,0:T(8,128)(2,1)S(1)}, u32[]{:S(2)}, u32[]{:S(2)}) collective-permute-start(s16[2064,128]{1,0:T(8,128)(2,1)S(1)} %copy-done.6), channel_id=1, source_target_pairs={{4,8},{8,4},{5,9},{9,5},{6,10},{10,6},{7,11},{11,7},{20,24},{24,20... | collective-permute-start | bytes 1585160 | tf_op jit(solution)/shard_map/ppermute | solution.py:735
  260.3 14.6 %collective-permute-start.31 = (s16[2064,128]{1,0:T(8,128)(2,1)}, s16[2064,128]{1,0:T(8,128)(2,1)S(1)}, u32[]{:S(2)}, u32[]{:S(2)}) collective-permute-start(s16[2064,128]{1,0:T(8,128)(2,1)} %add_chunk.26.a.refs_0_), channel_id=1, source_target_pairs={{4,8},{8,4},{5,9},{9,5},{6,10},{10,6},{7,11},{11,7},{20,24},{24,20... | collective-permute-start | bytes 1585160 | tf_op jit(solution)/shard_map/ppermute | solution.py:735
  268.0 18.1 %collective-permute-start.42 = (s16[2064,128]{1,0:T(8,128)(2,1)S(1)}, s16[2064,128]{1,0:T(8,128)(2,1)S(1)}, u32[]{:S(2)}, u32[]{:S(2)}) collective-permute-start(s16[2064,128]{1,0:T(8,128)(2,1)S(1)} %copy-done.1), channel_id=1, source_target_pairs={{4,0},{8,12},{5,1},{9,13},{6,2},{10,14},{7,3},{11,15},{20,16},{24,... | collective-permute-start | bytes 1585160 | tf_op jit(solution)/shard_map/ppermute | solution.py:740
  269.4 28.1 %collective-permute-start.43 = (s16[2064,128]{1,0:T(8,128)(2,1)S(1)}, s16[2064,128]{1,0:T(8,128)(2,1)S(1)}, u32[]{:S(2)}, u32[]{:S(2)}) collective-permute-start(s16[2064,128]{1,0:T(8,128)(2,1)S(1)} %copy-done.5), channel_id=1, source_target_pairs={{4,0},{8,12},{5,1},{9,13},{6,2},{10,14},{7,3},{11,15},{20,16},{24,... | collective-permute-start | bytes 1585160 | tf_op jit(solution)/shard_map/ppermute | solution.py:740
  270.9 37.9 %collective-permute-start.41 = (s16[2064,128]{1,0:T(8,128)(2,1)S(1)}, s16[2064,128]{1,0:T(8,128)(2,1)S(1)}, u32[]{:S(2)}, u32[]{:S(2)}) collective-permute-start(s16[2064,128]{1,0:T(8,128)(2,1)S(1)} %copy-done.2), channel_id=1, source_target_pairs={{4,0},{8,12},{5,1},{9,13},{6,2},{10,14},{7,3},{11,15},{20,16},{24,... | collective-permute-start | bytes 1585160 | tf_op jit(solution)/shard_map/ppermute | solution.py:740
  274.9 45.2 %collective-permute-start.40 = (s16[2064,128]{1,0:T(8,128)(2,1)S(1)}, s16[2064,128]{1,0:T(8,128)(2,1)S(1)}, u32[]{:S(2)}, u32[]{:S(2)}) collective-permute-start(s16[2064,128]{1,0:T(8,128)(2,1)S(1)} %copy-done.4), channel_id=1, source_target_pairs={{4,0},{8,12},{5,1},{9,13},{6,2},{10,14},{7,3},{11,15},{20,16},{24,... | collective-permute-start | bytes 1585160 | tf_op jit(solution)/shard_map/ppermute | solution.py:740
  279.0 52.4 %collective-permute-start.39 = (s16[2064,128]{1,0:T(8,128)(2,1)S(1)}, s16[2064,128]{1,0:T(8,128)(2,1)S(1)}, u32[]{:S(2)}, u32[]{:S(2)}) collective-permute-start(s16[2064,128]{1,0:T(8,128)(2,1)S(1)} %copy-done.3), channel_id=1, source_target_pairs={{4,0},{8,12},{5,1},{9,13},{6,2},{10,14},{7,3},{11,15},{20,16},{24,... | collective-permute-start | bytes 1585160 | tf_op jit(solution)/shard_map/ppermute | solution.py:740
  286.1 56.6 %collective-permute-start.38 = (s16[2064,128]{1,0:T(8,128)(2,1)S(1)}, s16[2064,128]{1,0:T(8,128)(2,1)S(1)}, u32[]{:S(2)}, u32[]{:S(2)}) collective-permute-start(s16[2064,128]{1,0:T(8,128)(2,1)S(1)} %copy-done.9), channel_id=1, source_target_pairs={{4,0},{8,12},{5,1},{9,13},{6,2},{10,14},{7,3},{11,15},{20,16},{24,... | collective-permute-start | bytes 1585160 | tf_op jit(solution)/shard_map/ppermute | solution.py:740
  297.5 56.3 %collective-permute-start.36 = (s16[2064,128]{1,0:T(8,128)(2,1)}, s16[2064,128]{1,0:T(8,128)(2,1)S(1)}, u32[]{:S(2)}, u32[]{:S(2)}) collective-permute-start(s16[2064,128]{1,0:T(8,128)(2,1)} %add_chunk.30.refs_1_.total), channel_id=1, source_target_pairs={{4,0},{8,12},{5,1},{9,13},{6,2},{10,14},{7,3},{11,15},{20,16},{24,... | collective-permute-start | bytes 1585160 | tf_op jit(solution)/shard_map/ppermute | solution.py:740
  308.8 50.6 %collective-permute-start.32 = (s16[2064,128]{1,0:T(8,128)(2,1)S(1)}, s16[2064,128]{1,0:T(8,128)(2,1)S(1)}, u32[]{:S(2)}, u32[]{:S(2)}) collective-permute-start(s16[2064,128]{1,0:T(8,128)(2,1)S(1)} %copy-done.8), channel_id=1, source_target_pairs={{4,0},{8,12},{5,1},{9,13},{6,2},{10,14},{7,3},{11,15},{20,16},{24,... | collective-permute-start | bytes 1585160 | tf_op jit(solution)/shard_map/ppermute | solution.py:740
  (67 other events, 571.8 us)
